TPU v7x, 256 devices: a whole 4x4x8 slice. The times are simulated.
256 devices in a mesh: group: 4 (over y), dev: 64 (over x, z, core).
Axes of the slice: x: 4, y: 4, z: 8, core: 2. Of those that a mesh axis runs over, the one named last changes fastest.
Arguments:
- embeddings: bfloat16 [131072, 768], P(('group', 'dev')), may hold values from -6 to 6
- cluster: int32 [131072], P(('group', 'dev')), may hold values from 0 to 31, as said below
- order: int32 [131072], P(('group', 'dev')), may hold values from 0 to 131071, as said below
- query_local: int32 [16384], P(('group', 'dev')), may hold values from 0 to 511, as said below
Outputs:
- best: float32 [16384], P(('group', 'dev'))
Inputs may be any that keep to these rules, and one draw needn't show every extreme that they name: Each value is a cluster of 0 to 31; among the rows of one data owner (aligned blocks of 512 rows), at most 256 lie in clusters with one value of cluster modulo 4, and in every block some residue has exactly 256. `order`: all values are distinct: a permutation of 0 to 131071. `query_local`: each aligned block of 64 entries holds distinct row indices of one data owner; its i-th run of 16 entries names rows whose cluster modulo 4 equals i.
All inputs are finite; a program needn't handle non-finite values.
Results may differ from a plain program's by a relative error of at most 0.0013.
Values may be sent and summed in bfloat16 or wider, within the bound.
A program may use at most 128 MiB of HBM per device.

v0:
```python
import math

import jax
import jax.numpy as jnp
from jax import lax
from jax.sharding import PartitionSpec as P


def normalize(rows):
    wide = rows.astype(jnp.float32)
    total = jnp.sum(wide * wide, axis=-1)
    return (wide * lax.rsqrt(total + 1e-06)[:, None]).astype(jnp.bfloat16)


def tile_best(rows, clu_rows, ord_rows, keys, key_clu, key_ord):
    scores = lax.dot_general(
        rows, keys, (((1,), (1,)), ((), ())), preferred_element_type=jnp.float32
    )
    keep = (
        (clu_rows[:, None] == key_clu[None, :])
        & (key_ord[None, :] < ord_rows[:, None])
        & (key_clu[None, :] >= 0)
    )
    return jnp.max(jnp.where(keep, scores, jnp.float32(-1.0)), axis=1)


def best_against(queries, query_clu, query_ord, keys, key_clu, key_ord):
    count = queries.shape[0]
    width = math.gcd(count, 1024)

    def one_block(items):
        rows, clu_rows, ord_rows = items
        return tile_best(rows, clu_rows, ord_rows, keys, key_clu, key_ord)

    blocked = (
        queries.reshape(count // width, width, queries.shape[1]),
        query_clu.reshape(count // width, width),
        query_ord.reshape(count // width, width),
    )
    return lax.map(one_block, blocked).reshape(count)


def body(embeddings, cluster, order, query_local):
    unit = normalize(embeddings)
    own_rows = unit[query_local]
    own_clu = cluster[query_local]
    own_ord = order[query_local]
    per_device = query_local.shape[0]
    every_rows, every_clu, every_ord = (
        lax.all_gather(own_rows, ("group", "dev"), axis=0, tiled=True),
        lax.all_gather(own_clu, ("group", "dev"), axis=0, tiled=True),
        lax.all_gather(own_ord, ("group", "dev"), axis=0, tiled=True),
    )
    partial_value = best_against(every_rows, every_clu, every_ord, unit, cluster, order)
    total = lax.pmax(partial_value, ("group", "dev"))
    best = lax.dynamic_slice_in_dim(
        total, lax.axis_index(("group", "dev")) * per_device, per_device
    )
    return best


def solution(mesh):
    return jax.shard_map(
        body,
        mesh=mesh,
        in_specs=(
            P(("group", "dev"), None),
            P(("group", "dev")),
            P(("group", "dev")),
            P(("group", "dev")),
        ),
        out_specs=P(("group", "dev")),
        check_vma=False,
    )
```

profile of v0, /device:TPU:1, one launch (start us, length us, event | category | flops | bytes accessed | tf_op | source)
XLA Modules:
  0.0 684.5 jit_solution(16409740063601307738)
XLA Ops:
  6.5 0.7 compare_select_fusion
  7.3 1.5 gather_fusion
  8.8 1.5 gather_fusion.1
  10.3 0.3 dynamic-update-slice
  10.6 0.3 dynamic-update-slice.1
  10.9 0.3 copy-done.4
  11.2 0.3 copy-done.3
  11.6 1.4 fusion.3
  13.0 0.2 fusion.4
  13.2 1.3 gather_fusion.2
  14.6 243.0 %all-reduce.8.cloned.1.call-done = (s32[16384]{0:T(1024)}, s32[16384]{0:T(1024)}) async-done(((s32[16384]{0:T(1024)}, s32[16384]{0:T(1024)}), (s32[16384]{0:T(1024)}, s32[16384]{0:T(1024)})) %all-reduce.8.cloned.1.call-update) | async-done | bytes 131088
  257.5 0.9 reshape.26
  258.4 0.9 reshape.27
  259.3 138.0 %all-gather.5.cloned.1.call-done = bf16[16384,768]{1,0:T(8,128)(2,1)} async-done(((bf16[64,768]{1,0:T(8,128)(2,1)}), bf16[16384,768]{1,0:T(8,128)(2,1)}) %all-gather.5.cloned.1.call-update) | async-done | bytes 25165840 | tf_op jit(solution)/shard_map/all_gather | solution.py:50
  397.3 43.9 %while.10 = (s32[]{:T(128)}, f32[16,1024]{1,0:T(8,128)S(1)}, s32[16,1024]{1,0:T(8,128)S(1)}, s32[512]{0:T(512)S(1)}, s32[512]{0:T(512)S(1)}, /*index=5*/s32[16,1...) while((s32[]{:T(128)}, f32[16,1024]{1,0:T(8,128)S(1)}, ...), condition=%wide.region_3.4_spmd, body=%wide.region_1.3_spmd.sunk | while | flops 808451584 | bytes 2403949 | solution.py:40
  397.3 2.6 select_reduce_fusion.2
  399.9 0.1 dynamic_update_slice.5
  400.1 2.6 select_reduce_fusion.2
  402.6 0.1 dynamic_update_slice.5
  402.8 2.6 select_reduce_fusion.2
  405.4 0.1 dynamic_update_slice.5
  405.6 2.6 select_reduce_fusion.2
  408.1 0.1 dynamic_update_slice.5
  408.3 2.6 select_reduce_fusion.2
  410.9 0.1 dynamic_update_slice.5
  411.0 2.6 select_reduce_fusion.2
  413.6 0.1 dynamic_update_slice.5
  413.8 2.6 select_reduce_fusion.2
  416.4 0.1 dynamic_update_slice.5
  416.5 2.6 select_reduce_fusion.2
  419.1 0.1 dynamic_update_slice.5
  419.3 2.6 select_reduce_fusion.2
  421.8 0.1 dynamic_update_slice.5
  422.0 2.6 select_reduce_fusion.2
  424.6 0.1 dynamic_update_slice.5
  424.7 2.6 select_reduce_fusion.2
  427.3 0.1 dynamic_update_slice.5
  427.5 2.6 select_reduce_fusion.2
  430.1 0.1 dynamic_update_slice.5
  430.2 2.6 select_reduce_fusion.2
  432.8 0.1 dynamic_update_slice.5
  433.0 2.6 select_reduce_fusion.2
  435.6 0.1 dynamic_update_slice.5
  435.7 2.6 select_reduce_fusion.2
  438.5 2.6 select_reduce_fusion.2
  441.2 0.6 copy.5
  441.8 234.9 %all-reduce.6.cloned.1.call-done = f32[16384]{0:T(1024)} async-done(((f32[16384]{0:T(1024)}), f32[16384]{0:T(1024)}) %all-reduce.6.cloned.1.call-update) | async-done | bytes 65552 | tf_op jit(solution)/shard_map/pmax | solution.py:55
  676.7 1.3 dynamic_slice.14
  (53 shorter events, 0.7 us)
Async XLA Ops:
  6.5 6.4 copy-start.2
  6.5 251.0 %all-reduce.8.cloned.1.call-start = ((), (), s32[]{:S(2)}) async-start(), calls=%async_computation.2 | async-start | bytes 262144
  8.8 388.5 %copy-start = (s32[512]{0:T(512)S(1)}, s32[512]{0:T(512)}, u32[]{:S(2)}) copy-start(s32[512]{0:T(512)} %param.7) | copy-start | bytes 6148
  8.8 388.5 %copy-start.1 = (s32[512]{0:T(512)S(1)}, s32[512]{0:T(512)}, u32[]{:S(2)}) copy-start(s32[512]{0:T(512)} %param.8) | copy-start | bytes 6148
  10.6 0.6 copy-start.4
  10.9 0.6 copy-start.3
  11.5 385.8 %all-gather.5.cloned.1.call-start = ((), (), s32[]{:S(2)}) async-start(), calls=%async_computation.1 | async-start | bytes 25264128 | tf_op jit(solution)/shard_map/all_gather | solution.py:50
  14.5 662.2 %all-reduce.6.cloned.1.call-start = ((), (), s32[]{:S(2)}) async-start(), calls=%async_computation | async-start | bytes 131072 | tf_op jit(solution)/shard_map/pmax | solution.py:55
Sparse Core Ops, SparseCore 0:
  13.0 244.5 all-reduce.7
  261.4 135.8 all-gather.4
  441.9 234.6 all-reduce.5
where the time goes:
time: 685 us; the launch traced here: 684 us
  waiting for transfers between devices  616 us (90%)
  matrix products  41.1 us (6%)
  between operations  13.2 us (2%)
  local copies, waits for them, and re-layouts  11.2 us (2%)
    unnamed x4, waiting for transfers between devices  243 us
    pmax x1, waiting for transfers between devices, body(): total = lax.pmax(partial_value, ('group', 'dev'))  235 us
    all_gather x1, waiting for transfers between devices, body(): lax.all_gather(own_rows, ('group', 'dev'), axis=0, tiled=True)  138 us
    dot_general x16, matrix products, tile_best(): lax.dot_general(rows, keys, (((1,), (1,)), ((), ())), preferred_element_t...  41.1 us
  transfers between devices with their start and end apart: 3, of which 3 were waited for; matrix products, arithmetic and copies ran while one was open for 1% of the time, Pallas kernels for 0%

commit v1 on v0

v1 whole, which is shorter than its diff:
```python
import jax
import jax.numpy as jnp
from jax import lax
from jax.experimental import pallas as pl
from jax.experimental.pallas import tpu as pltpu
from jax.sharding import PartitionSpec as P

MESH = pl.DeviceIdType.MESH
F32, BF16 = jnp.float32, jnp.bfloat16
NY, NX, NZ = 4, 4, 8
D = 768
ROWS = 512
QB = 64
RUN = 16
CAP = 256
SPAN = 131072.0


def iota(shape, axis):
    return lax.broadcasted_iota(jnp.int32, shape, axis)


def meta_tile(picked):
    order = picked[1:2] + 256.0 * picked[2:3] + 65536.0 * picked[3:4]
    return jnp.where(iota(picked.shape, 0) == 0, picked[0:1], order)


def kernel(
    emb_ref, clu_ref, ord_ref, qry_ref, out_ref,
    unit, qsel, qmsrc, qmrecv, ksel, kmsrc, kbuf, kmeta, kcode, qbuf, qmeta,
    best, zred, rtile, fin,
    s_qy, s_my, r_qy, r_my, s_k, s_km, r_k, r_km, s_kf, s_kmf,
    s_g, s_gm, r_g, r_gm, s_z, r_z, s_f, r_f,
):
    y = lax.axis_index("group")
    d = lax.axis_index("dev")
    x, z, c = d // (2 * NZ), (d // 2) % NZ, d % 2

    def peer(dy=0, dx=0, dz=0, dc=0):
        return (
            (y + dy) % NY,
            (((x + dx) % NX) * NZ + (z + dz) % NZ) * 2 + (c + dc) % 2,
        )

    def rcopy(src, dst, ssem, rsem, to):
        return pltpu.make_async_remote_copy(
            src_ref=src, dst_ref=dst, send_sem=ssem, recv_sem=rsem,
            device_id=to, device_id_type=MESH,
        )

    barrier = pltpu.get_barrier_semaphore()
    greeted = [peer(dz=k) for k in range(1, NZ)] + [peer(dc=1)]
    greeted += [peer(dy=k // NX, dx=k % NX) for k in range(1, NY * NX)]
    for to in greeted:
        pl.semaphore_signal(barrier, inc=1, device_id=to, device_id_type=MESH)

    wide = emb_ref[...].astype(F32)
    total = jnp.sum(wide * wide, axis=-1, keepdims=True)
    unit[...] = (wide * lax.rsqrt(total + 1e-06)).astype(BF16)

    clu, order = clu_ref[...], ord_ref[...]
    row = iota((8, ROWS), 0)
    digits = jnp.where(
        row == 0,
        clu + 1,
        jnp.where(
            row == 1,
            order & 255,
            jnp.where(row == 2, (order >> 8) & 255, jnp.where(row == 3, order >> 16, 0)),
        ),
    ).astype(F32).astype(BF16)

    lanes = jnp.concatenate([qry_ref[...], qry_ref[...]], axis=1).astype(F32)
    column = jnp.transpose(jnp.broadcast_to(lanes, (128, 128)))[:QB]
    column = jnp.concatenate([column] * (ROWS // 128), axis=1)
    pick = jnp.where(column == iota((QB, ROWS), 1).astype(F32), 1.0, 0.0).astype(BF16)
    qsel[...] = jnp.dot(pick, unit[...], preferred_element_type=F32).astype(BF16)
    picked = lax.dot_general(digits, pick, (((1,), (1,)), ((), ())), preferred_element_type=F32)
    picked = meta_tile(jnp.concatenate([picked, picked], axis=1))
    lane = iota((8, 128), 1)
    for i in range(NY):
        tile = jnp.where((lane // RUN) % NY == i, picked, 0.0)
        tile = tile + pltpu.roll(tile, RUN, 1)
        qmsrc[i] = tile + pltpu.roll(tile, 2 * RUN, 1)

    pl.semaphore_wait(barrier, len(greeted))

    def run_at(which):
        return pl.ds(pl.multiple_of(which * RUN, RUN), RUN)

    def block_at(which):
        return pl.ds(pl.multiple_of(which * QB, QB), QB)

    here = pl.ds(pl.multiple_of(x * QB + y * RUN, RUN), RUN)
    for k in range(1, NY):
        i = (y + k) % NY
        rcopy(qsel.at[run_at(i)], qbuf.at[z, here], s_qy.at[k], r_qy.at[y], peer(dy=k)).start()
        rcopy(qmsrc.at[i], qmrecv.at[y], s_my.at[k], r_my.at[y], peer(dy=k)).start()
    qbuf[z, here] = qsel[run_at(y)]
    qmrecv[y] = qmsrc[y]

    residue = clu % NY
    member = jnp.where(row == residue, 1.0, 0.0)
    before = jnp.where(iota((ROWS, ROWS), 0) < iota((ROWS, ROWS), 1), 1.0, 0.0).astype(BF16)
    prefix = jnp.dot(member.astype(BF16), before, preferred_element_type=F32)
    rank = jnp.sum(member * prefix, axis=0, keepdims=True)
    dest = residue.astype(F32) * CAP + rank
    slot = iota((CAP, ROWS), 0)

    def of_residue(r):
        place = jnp.where((slot + r * CAP).astype(F32) == dest, 1.0, 0.0).astype(BF16)
        rows = jnp.dot(place, unit[...], preferred_element_type=F32).astype(BF16)
        tile = lax.dot_general(digits, place, (((1,), (1,)), ((), ())), preferred_element_type=F32)
        return rows, meta_tile(tile)

    def half(which):
        return pl.ds(pl.multiple_of(which * CAP, CAP), CAP)

    def key_send(k):
        to = peer(dy=k)
        rcopy(ksel.at[k], kbuf.at[y, half(c)], s_k.at[k], r_k.at[y, c], to).start()
        rcopy(kmsrc.at[k], kmeta.at[y, c], s_km.at[k], r_km.at[y, c], to).start()

    def key_select(k):
        rows, tile = of_residue((y + k) % NY)
        ksel[k] = rows
        kmsrc[k] = tile

    def key_wait(ys, cs):
        rcopy(kbuf.at[ys, half(cs)], kbuf.at[ys, half(cs)], s_kf.at[0], r_k.at[ys, cs], peer(dc=1)).wait_recv()
        rcopy(kmeta.at[ys, cs], kmeta.at[ys, cs], s_kmf.at[0], r_km.at[ys, cs], peer(dc=1)).wait_recv()

    def key_share(k):
        ys = (y + k) % NY
        at = kbuf.at[ys, half(c)]
        rcopy(at, at, s_kf.at[k], r_k.at[ys, c], peer(dc=1)).start()
        rcopy(kmeta.at[ys, c], kmeta.at[ys, c], s_kmf.at[k], r_km.at[ys, c], peer(dc=1)).start()

    def key_codes(k):
        ys = (y + k) % NY
        for cs in range(2):
            tile = kmeta[ys, cs]
            code = (tile[0:1] - 1.0) * SPAN + tile[1:2]
            kcode[ys, cs * CAP:(cs + 1) * CAP, :] = jnp.transpose(jnp.broadcast_to(code, (128, CAP)))

    for k in (1, 3, 2):
        key_select(k)
        key_send(k)
    rows, tile = of_residue(y)
    kbuf[y, half(c)] = rows
    kmeta[y, c] = tile
    key_share(0)

    for k in range(1, NY):
        ys = (y + k) % NY
        at = pl.ds(pl.multiple_of(x * QB + ys * RUN, RUN), RUN)
        rcopy(qsel.at[run_at(ys)], qbuf.at[z, at], s_qy.at[k], r_qy.at[ys], peer(dy=k)).wait_recv()
        rcopy(qmsrc.at[ys], qmrecv.at[ys], s_my.at[k], r_my.at[ys], peer(dy=k)).wait_recv()
    own = qmrecv[0]
    for i in range(1, NY):
        own = jnp.where((lane // RUN) % NY == i, qmrecv[i], own)
    qmeta[z, x] = own

    def block(dx, dz):
        return (x + dx) % NX, (z + dz) % NZ

    def send(count, at, to):
        xs, zs = at
        n = count[0]
        count[0] += 1
        rows = qbuf.at[zs, block_at(xs)]
        rcopy(rows, rows, s_g.at[n], r_g.at[zs, xs], to).start()
        tile = qmeta.at[zs, xs]
        rcopy(tile, tile, s_gm.at[n], r_gm.at[zs, xs], to).start()

    def arrive(at):
        xs, zs = at
        rows = qbuf.at[zs, block_at(xs)]
        rcopy(rows, rows, s_g.at[0], r_g.at[zs, xs], peer(dc=1)).wait_recv()
        tile = qmeta.at[zs, xs]
        rcopy(tile, tile, s_gm.at[0], r_gm.at[zs, xs], peer(dc=1)).wait_recv()

    def along_x(count, at):
        for dx in (1, 3, 2):
            send(count, at, peer(dx=dx))

    sent = ([0], [0])

    def x_start():
        count = sent[0]
        along_x(count, block(0, 0))
        send(count, block(0, 0), peer(dz=1))
        send(count, block(0, 0), peer(dz=-1))
        for dx in (1, 3, 2):
            arrive(block(dx, 0))
            send(count, block(dx, 0), peer(dz=1))
            send(count, block(dx, 0), peer(dz=-1))

    def turn(dx):
        return 1 - 2 * (((x + dx) % NX) % 2)

    def x_step(s):
        count = sent[0]
        for dx in range(NX):
            if s == 4:
                arrive(block(dx, 4))
                continue
            arrive(block(dx, -s))
            if s < 3:
                send(count, block(dx, -s), peer(dz=1))
            arrive(block(dx, s))
            if s < 3:
                send(count, block(dx, s), peer(dz=-1))
            else:
                send(count, block(dx, -3 * turn(dx)), peer(dz=turn(dx)))

    def z_start():
        count = sent[1]
        send(count, block(0, 0), peer(dz=1))
        send(count, block(0, 0), peer(dz=-1))
        along_x(count, block(0, 0))
        x_wait(0)

    def z_step(s):
        count = sent[1]
        if s == 4:
            arrive(block(0, 4))
            along_x(count, block(0, 4))
            return
        arrive(block(0, -s))
        if s < 3:
            send(count, block(0, -s), peer(dz=1))
        along_x(count, block(0, -s))
        arrive(block(0, s))
        if s < 3:
            send(count, block(0, s), peer(dz=-1))
        else:
            send(count, block(0, -3 * turn(0)), peer(dz=turn(0)))
        along_x(count, block(0, s))

    def x_wait(s):
        for dz in ((s,) if s in (0, 4) else (-s, s)):
            for dx in (1, 3, 2):
                arrive(block(dx, dz))

    def by_core(first, second):
        pl.when(c == 0)(first)
        pl.when(c == 1)(second)

    def slab(i):
        return (z + NZ + (1 - 2 * (i % 2)) * ((i + 1) // 2)) % NZ

    def score(i, j):
        zs = slab(i)
        ys = (y + j + (j // 2) * (5 - 2 * j)) % NY
        s = lax.dot_general(kbuf[ys], qbuf[zs], (((1,), (1,)), ((), ())), preferred_element_type=F32)
        code = kcode[ys]
        for p in range(2):
            tile = jnp.where(lane < QB, qmeta[zs, 2 * p], qmeta[zs, 2 * p + 1])
            low = (tile[0:1] - 1.0) * SPAN
            high = low + tile[1:2]
            keep = (code >= low) & (code < high)
            top = jnp.max(jnp.where(keep, s[:, p * 128:(p + 1) * 128], -1.0), axis=0, keepdims=True)
            best[zs, p:p + 1, :] = jnp.maximum(best[zs, p:p + 1, :], top)

    def rect(i0, i1, j0, j1):
        nj = j1 - j0

        def one(t, carry):
            score(i0 + t // nj, j0 + t % nj)
            return carry

        lax.fori_loop(0, (i1 - i0) * nj, one, 0)

    def slab_copy(i):
        zs = slab(i)
        return rcopy(best.at[zs], zred.at[z], s_z.at[i], r_z.at[z], (y, (x * NZ + zs) * 2 + c))

    best[...] = jnp.full(best.shape, -1.0, F32)

    by_core(x_start, z_start)
    key_wait(y, 1 - c)
    key_codes(0)
    rect(0, 1, 0, 1)

    def z_two():
        z_step(1)
        z_step(2)
        x_wait(1)

    by_core(lambda: x_step(1), z_two)
    rect(1, 3, 0, 1)
    for k in (1, 3):
        key_wait((y + k) % NY, c)
        key_share(k)
    for k in (1, 3):
        key_wait((y + k) % NY, 1 - c)
        key_codes(k)
    rect(0, 3, 1, 3)

    def z_three():
        z_step(3)
        x_wait(2)

    by_core(lambda: x_step(2), z_three)
    rect(3, 5, 0, 3)

    def z_four():
        z_step(4)
        x_wait(3)

    by_core(lambda: x_step(3), z_four)
    rect(5, 7, 0, 3)
    key_wait((y + 2) % NY, c)
    key_share(2)
    key_wait((y + 2) % NY, 1 - c)
    key_codes(2)
    rect(0, 7, 3, 4)
    for i in range(1, 7):
        slab_copy(i).start()
    by_core(lambda: x_step(4), lambda: x_wait(4))
    rect(7, 8, 0, 4)
    slab_copy(7).start()

    top = best[z]
    for k in range(1, NZ):
        zs = (z + k) % NZ
        rcopy(best.at[zs], zred.at[zs], s_z.at[0], r_z.at[zs], peer(dz=k)).wait_recv()
        top = jnp.maximum(top, zred[zs])
    rtile[...] = top
    for k in range(1, NY * NX):
        to = peer(dy=k // NX, dx=k % NX)
        rcopy(rtile, fin.at[y, x], s_f.at[k], r_f.at[y, x], to).start()
    fin[y, x] = top
    for k in range(1, NY * NX):
        ys, xs = (y + k // NX) % NY, (x + k % NX) % NX
        rcopy(rtile, fin.at[ys, xs], s_f.at[0], r_f.at[ys, xs], peer(dy=k // NX, dx=k % NX)).wait_recv()
    result = jnp.zeros((8, 128), F32)
    for r in range(NY):
        tile = jnp.maximum(jnp.maximum(fin[r, 0], fin[r, 1]), jnp.maximum(fin[r, 2], fin[r, 3]))
        tile = jnp.where(x // 2 == 0, tile[0:1], tile[1:2])
        tile = jnp.broadcast_to(tile, (8, 128))
        tile = pltpu.roll(tile, (r * RUN - (x % 2) * QB - y * RUN + 256) % 128, 1)
        result = jnp.where(lane // RUN == r, tile, result)
    out_ref[...] = result[0:1, 0:QB]

    for k in range(1, NY):
        to = peer(dy=k)
        rcopy(qsel.at[pl.ds(0, RUN)], qbuf.at[z, here], s_qy.at[k], r_qy.at[y], to).wait_send()
        rcopy(qmsrc.at[0], qmrecv.at[0], s_my.at[k], r_my.at[y], to).wait_send()
        rcopy(ksel.at[k], kbuf.at[y, half(c)], s_k.at[k], r_k.at[y, c], to).wait_send()
        rcopy(kmsrc.at[k], kmeta.at[y, c], s_km.at[k], r_km.at[y, c], to).wait_send()
    for k in range(NY):
        at = kbuf.at[y, half(c)]
        rcopy(at, at, s_kf.at[k], r_k.at[y, c], peer(dc=1)).wait_send()
        rcopy(kmeta.at[y, c], kmeta.at[y, c], s_kmf.at[k], r_km.at[y, c], peer(dc=1)).wait_send()
    for n in range(31):
        rows = qbuf.at[z, block_at(x)]
        rcopy(rows, rows, s_g.at[n], r_g.at[z, x], peer(dc=1)).wait_send()
        tile = qmeta.at[z, x]
        rcopy(tile, tile, s_gm.at[n], r_gm.at[z, x], peer(dc=1)).wait_send()
    for i in range(1, NZ):
        slab_copy(i).wait_send()
    for k in range(1, NY * NX):
        rcopy(rtile, fin.at[y, x], s_f.at[k], r_f.at[y, x], peer(dy=k // NX, dx=k % NX)).wait_send()


def body(embeddings, cluster, order, query_local):
    dma = pltpu.SemaphoreType.DMA
    out = pl.pallas_call(
        kernel,
        out_shape=jax.ShapeDtypeStruct((1, QB), F32),
        in_specs=[pl.BlockSpec(memory_space=pltpu.VMEM)] * 4,
        out_specs=pl.BlockSpec(memory_space=pltpu.VMEM),
        scratch_shapes=[
            pltpu.VMEM((ROWS, D), BF16),
            pltpu.VMEM((QB, D), BF16),
            pltpu.VMEM((NY, 8, 128), F32),
            pltpu.VMEM((NY, 8, 128), F32),
            pltpu.VMEM((NY, CAP, D), BF16),
            pltpu.VMEM((NY, 8, CAP), F32),
            pltpu.VMEM((NY, 2 * CAP, D), BF16),
            pltpu.VMEM((NY, 2, 8, CAP), F32),
            pltpu.VMEM((NY, 2 * CAP, 128), F32),
            pltpu.VMEM((NZ, NX * QB, D), BF16),
            pltpu.VMEM((NZ, NX, 8, 128), F32),
            pltpu.VMEM((NZ, 8, 128), F32),
            pltpu.VMEM((NZ, 8, 128), F32),
            pltpu.VMEM((8, 128), F32),
            pltpu.VMEM((NY, NX, 8, 128), F32),
            dma((NY,)), dma((NY,)), dma((NY,)), dma((NY,)),
            dma((NY,)), dma((NY,)), dma((NY, 2)), dma((NY, 2)), dma((NY,)), dma((NY,)),
            dma((31,)), dma((31,)), dma((NZ, NX)), dma((NZ, NX)),
            dma((NZ,)), dma((NZ,)), dma((NY * NX,)), dma((NY, NX)),
        ],
        compiler_params=pltpu.CompilerParams(
            collective_id=0, has_side_effects=True, vmem_limit_bytes=48 * 1024 * 1024
        ),
        name="dedup",
    )(
        embeddings,
        cluster.reshape(1, ROWS),
        order.reshape(1, ROWS),
        query_local.reshape(1, QB),
    )
    return out.reshape(QB)


def solution(mesh):
    return jax.shard_map(
        body,
        mesh=mesh,
        in_specs=(
            P(("group", "dev"), None),
            P(("group", "dev")),
            P(("group", "dev")),
            P(("group", "dev")),
        ),
        out_specs=P(("group", "dev")),
        check_vma=False,
    )
```

time: 685 us -> 63.8 us (0.09)
  waiting for transfers between devices: 616 us -> 0 us
  Pallas kernels: 0 us -> 61.3 us
  matrix products: 41.1 us -> 0 us
  between operations: 13.2 us -> 0.02 us
  local copies, waits for them, and re-layouts: 11.2 us -> 2.34 us
    unnamed x4 -> x0, waiting for transfers between devices: 243 us -> none
    pmax x1 -> x0, waiting for transfers between devices: 235 us -> none  [body(): total = lax.pmax(partial_value, ('group', 'dev'))]
    all_gather x1 -> x0, waiting for transfers between devices: 138 us -> none  [body(): lax.all_gather(own_rows, ('group', 'dev'), axis=0, tiled=True)]
    pallas_call x0 -> x1, Pallas kernels: none -> 61.3 us  [body(): pl.pallas_call(kernel, out_shape=jax.ShapeDtypeStruct((1, QB), F32), in_s...]
    dot_general x16 -> x0, matrix products: 41.1 us -> none  [tile_best(): lax.dot_general(rows, keys, (((1,), (1,)), ((), ())), preferred_element_t...]
  transfers between devices with their start and end apart: 3 -> 0, of which waited for: 3 -> 0; matrix products, arithmetic and copies ran while one was open for 1% -> 0% of each run, Pallas kernels for 0% -> 0%
where the time goes in v1:
time: 63.8 us; the launch traced here: 63.7 us
  Pallas kernels  61.3 us (96%)
  local copies, waits for them, and re-layouts  2.34 us (4%)
    pallas_call x1, Pallas kernels, body(): pl.pallas_call(kernel, out_shape=jax.ShapeDtypeStruct((1, QB), F32), in_s...  61.3 us
    unnamed x9, local copies, waits for them, and re-layouts  2.34 us

profile of v1, /device:TPU:1, one launch (start us, length us, event | category | flops | bytes accessed | tf_op | source)
XLA Modules:
  0.0 63.7 jit_solution(15461577310677415785)
XLA Ops:
  0.0 0.0 copy-start.2
  0.0 0.0 copy-start.1
  0.0 0.0 copy-start.3
  0.0 0.7 %copy-done.2 = s32[512]{0:T(512)S(1)} copy-done((s32[512]{0:T(512)S(1)}, s32[512]{0:T(512)}, u32[]{:S(2)}) %copy-start.2) | copy-done | bytes 2072
  0.7 0.0 copy-done.1
  0.7 0.0 copy-done.3
  0.7 0.0 copy-start
  0.7 1.1 %copy-done = bf16[512,768]{1,0:T(8,128)(2,1)S(1)} copy-done((bf16[512,768]{1,0:T(8,128)(2,1)S(1)}, bf16[512,768]{1,0:T(8,128)(2,1)}, u32[]{:S(2)}) %copy-start) | copy-done | bytes 786456
  1.8 61.3 %dedup.1 = f32[1,64]{1,0:T(1,128)S(1)} custom-call(bf16[512,768]{1,0:T(8,128)(2,1)S(1)} %copy-done, s32[1,512]{1,0:T(1,128)S(1)} %bitcast.4, s32[1,512]{1,0:T(1,128)S(1)} %bitcast.5, s32[1,64]{1,0:T(1,128)S(1)} %bitcast.6), custom_call_target="tpu_custom_call" | custom-call | tf_op jit(solution)/shard_map/dedup/pallas_call | solution.py:370
  63.2 0.5 copy.6
Async XLA Ops:
  0.0 0.7 %copy-start.2 = (s32[512]{0:T(512)S(1)}, s32[512]{0:T(512)}, u32[]{:S(2)}) copy-start(s32[512]{0:T(512)} %param.6) | copy-start | bytes 6148
  0.0 0.7 %copy-start.1 = (s32[512]{0:T(512)S(1)}, s32[512]{0:T(512)}, u32[]{:S(2)}) copy-start(s32[512]{0:T(512)} %param.5) | copy-start | bytes 6148
  0.0 0.7 %copy-start.3 = (s32[64]{0:T(128)S(1)}, s32[64]{0:T(128)}, u32[]{:S(2)}) copy-start(s32[64]{0:T(128)} %param.7) | copy-start | bytes 772
  0.7 1.1 %copy-start = (bf16[512,768]{1,0:T(8,128)(2,1)S(1)}, bf16[512,768]{1,0:T(8,128)(2,1)}, u32[]{:S(2)}) copy-start(bf16[512,768]{1,0:T(8,128)(2,1)} %emb_ref.1) | copy-start | bytes 2359300

commit v2 on v0

v2 whole, which is shorter than its diff:
```python
import jax
import jax.numpy as jnp
from jax import lax
from jax.experimental import pallas as pl
from jax.experimental.pallas import tpu as pltpu
from jax.sharding import PartitionSpec as P

MESH = pl.DeviceIdType.MESH
F32, BF16 = jnp.float32, jnp.bfloat16
NY, NX, NZ = 4, 4, 8
D = 768
ROWS = 512
QB = 64
RUN = 16
CAP = 256
SPAN = 131072.0


def iota(shape, axis):
    return lax.broadcasted_iota(jnp.int32, shape, axis)


def meta_tile(picked):
    order = picked[1:2] + 256.0 * picked[2:3] + 65536.0 * picked[3:4]
    return jnp.where(iota(picked.shape, 0) == 0, picked[0:1], order)


def kernel(
    emb_hbm, clu_hbm, ord_hbm, qry_hbm, out_ref,
    emb_ref, clu_ref, ord_ref, qry_ref,
    unit, qsel, qmsrc, qmrecv, ksel, kmsrc, kbuf, kmeta, kcode, qbuf, qmeta,
    best, zred, rtile, fin,
    s_in, s_q, s_m, r_q, r_m, s_k, s_km, r_k, r_km, s_kf, s_kmf,
    s_g, s_gm, r_g, r_gm, s_z, r_z, s_f, r_f, s_l, beside,
):
    y = lax.axis_index("group")
    d = lax.axis_index("dev")
    x, z, c = d // (2 * NZ), (d // 2) % NZ, d % 2

    loads = [
        pltpu.make_async_copy(src, dst, s_in.at[n])
        for n, (src, dst) in enumerate(
            ((qry_hbm, qry_ref), (clu_hbm, clu_ref), (ord_hbm, ord_ref), (emb_hbm, emb_ref))
        )
    ]
    for load in loads:
        load.start()

    def peer(dy=0, dx=0, dz=0, dc=0):
        return (
            (y + dy) % NY,
            (((x + dx) % NX) * NZ + (z + dz) % NZ) * 2 + (c + dc) % 2,
        )

    def rcopy(src, dst, ssem, rsem, to):
        return pltpu.make_async_remote_copy(
            src_ref=src, dst_ref=dst, send_sem=ssem, recv_sem=rsem,
            device_id=to, device_id_type=MESH,
        )

    def by_core(x_then_z, z_then_x):
        pl.when(c == 1)(x_then_z)
        pl.when(c == 0)(z_then_x)

    barrier = pltpu.get_barrier_semaphore()
    X_PEERS = [dict(dz=1), dict(dz=-1)] + [dict(dy=k // NX, dx=k % NX) for k in range(1, NY * NX)]
    Z_PEERS = [dict(dz=1), dict(dz=-1)] + [dict(dx=k) for k in range(1, NX)]
    Z_PEERS += [dict(dy=k, dz=dz) for k in range(1, NY) for dz in (0, 1, -1)]

    def greet(peers):
        for to in peers:
            pl.semaphore_signal(barrier, inc=1, device_id=peer(**to), device_id_type=MESH)

    by_core(lambda: greet(X_PEERS), lambda: greet(Z_PEERS + [dict(dc=1)]))

    def unit_of(rows):
        wide = rows.astype(F32)
        total = jnp.sum(wide * wide, axis=-1, keepdims=True)
        return (wide * lax.rsqrt(total + 1e-06)).astype(BF16)

    for load in loads[:3]:
        load.wait()
    clu, order = clu_ref[...], ord_ref[...]
    row = iota((8, ROWS), 0)
    digits = jnp.where(
        row == 0,
        clu + 1,
        jnp.where(
            row == 1,
            order & 255,
            jnp.where(row == 2, (order >> 8) & 255, jnp.where(row == 3, order >> 16, 0)),
        ),
    ).astype(F32).astype(BF16)

    lanes = jnp.concatenate([qry_ref[...], qry_ref[...]], axis=1).astype(F32)
    column = jnp.transpose(jnp.broadcast_to(lanes, (128, 128)))[:QB]
    column = jnp.concatenate([column] * (ROWS // 128), axis=1)
    pick = jnp.where(column == iota((QB, ROWS), 1).astype(F32), 1.0, 0.0).astype(BF16)
    picked = lax.dot_general(digits, pick, (((1,), (1,)), ((), ())), preferred_element_type=F32)
    picked = meta_tile(jnp.concatenate([picked, picked], axis=1))
    lane = iota((8, 128), 1)
    for i in range(NY):
        tile = jnp.where((lane // RUN) % NY == i, picked, 0.0)
        tile = tile + pltpu.roll(tile, RUN, 1)
        qmsrc[i] = (tile + pltpu.roll(tile, 2 * RUN, 1))[0:2]
    loads[3].wait()
    qsel[...] = unit_of(jnp.dot(pick, emb_ref[...], preferred_element_type=F32))

    by_core(
        lambda: pl.semaphore_wait(barrier, len(X_PEERS) + 1),
        lambda: pl.semaphore_wait(barrier, len(Z_PEERS)),
    )

    @pl.when(c == 1)
    def _():
        pl.semaphore_signal(beside, inc=1, device_id=peer(dc=1), device_id_type=MESH)

    AT = {0: 0, -1: 1, 1: 2, -2: 3, 2: 4, -3: 5, 3: 6, 4: 7, -4: 7}

    def run_at(which):
        return pl.ds(pl.multiple_of(which * RUN, RUN), RUN)

    def block_at(at, xs, k=0, size=QB):
        return qbuf.at[pl.ds(pl.multiple_of(at * NX * QB + xs * QB + k * RUN, RUN), size)]

    sent = {"x": 0, "z": 0}

    def send(who, dx, source, target, to):
        xs = (x + dx) % NX
        n = sent[who]
        sent[who] += 1
        rcopy(block_at(source, xs), block_at(target, xs), s_g.at[n], r_g.at[target, xs], to).start()
        rcopy(qmeta.at[source, xs], qmeta.at[target, xs], s_gm.at[n], r_gm.at[target, xs], to).start()

    def along_z(who, dx, dz, step):
        send(who, dx, AT[dz], AT[dz - step], peer(dz=step))

    def along_x(dz):
        for dx in (1, 3, 2):
            send("z", 0, AT[dz], AT[dz], peer(dx=dx))

    def across(who, dx):
        t = 1 - 2 * (((x + dx) % NX) % 2)
        send(who, dx, 5 + (1 - t) // 2, 7, peer(dz=t))

    def arrive(dx, dz):
        at, xs = AT[dz], (x + dx) % NX
        rcopy(block_at(at, xs), block_at(at, xs), s_g.at[0], r_g.at[at, xs], peer(dc=1)).wait_recv()
        rcopy(qmeta.at[at, xs], qmeta.at[at, xs], s_gm.at[0], r_gm.at[at, xs], peer(dc=1)).wait_recv()

    X_RUNS = [(k, dx) for dx in (2, 1, 3, 0) for k in (2, 1, 3, 0) if (k, dx) != (0, 0)]
    Z_RUNS = [(k, dz) for dz in (1, -1, 0) for k in (2, 1, 3, 0) if (k, dz) != (0, 0)]

    def run_send(n, k, at, slot, to):
        i, back = (y + k) % NY, (NY - k) % NY
        rcopy(qsel.at[run_at(i)], block_at(at, x, back, RUN), s_q.at[n], r_q.at[slot, back], to).start()
        rcopy(qmsrc.at[i], qmrecv.at[slot, back], s_m.at[n], r_m.at[slot, back], to).start()

    def runs_arrive(at, xs, slot, own):
        for k in (0, 1, 3, 2)[own:]:
            rcopy(qsel.at[pl.ds(0, RUN)], block_at(at, xs, k, RUN), s_q.at[0], r_q.at[slot, k], peer(dc=1)).wait_recv()
            rcopy(qmsrc.at[0], qmrecv.at[slot, k], s_m.at[0], r_m.at[slot, k], peer(dc=1)).wait_recv()
        tile = qmrecv[slot, 0]
        for k in range(1, NY):
            tile = jnp.where((lane[0:2] // RUN) % NY == k, qmrecv[slot, k], tile)
        qmeta[at, xs] = tile

    def x_runs():
        for n, (k, dx) in enumerate(X_RUNS):
            run_send(n, k, 0, x, peer(dy=k, dx=dx))
        qmrecv[x, 0] = qmsrc[y]

    def z_runs():
        for n, (k, dz) in enumerate(Z_RUNS):
            run_send(n, k, AT[-dz], AT[-dz], peer(dy=k, dz=dz))
        qmrecv[0, 0] = qmsrc[y]

    by_core(x_runs, z_runs)
    block_at(0, x, 0, RUN)[...] = qsel[run_at(y)]

    unit[...] = unit_of(emb_ref[...])
    residue = clu % NY
    member = jnp.where(row == residue, 1.0, 0.0)
    before = jnp.where(iota((ROWS, ROWS), 0) < iota((ROWS, ROWS), 1), 1.0, 0.0).astype(BF16)
    prefix = jnp.dot(member.astype(BF16), before, preferred_element_type=F32)
    rank = jnp.sum(member * prefix, axis=0, keepdims=True)
    dest = residue.astype(F32) * CAP + rank
    slot_of = iota((CAP, ROWS), 0)

    def of_residue(r):
        place = jnp.where((slot_of + r * CAP).astype(F32) == dest, 1.0, 0.0).astype(BF16)
        rows = jnp.dot(place, unit[...], preferred_element_type=F32).astype(BF16)
        tile = lax.dot_general(digits, place, (((1,), (1,)), ((), ())), preferred_element_type=F32)
        return rows, meta_tile(tile)[0:2]

    PLACE = {0: 0, 1: 1, 3: 2, 2: 3}

    def key_at(j, cs):
        return kbuf.at[pl.ds(pl.multiple_of(j * 2 * CAP + cs * CAP, CAP), CAP)]

    def key_send(k):
        j, to = PLACE[k], peer(dy=k)
        rcopy(ksel.at[k], key_at(j, c), s_k.at[k], r_k.at[j, c], to).start()
        rcopy(kmsrc.at[k], kmeta.at[j, c], s_km.at[k], r_km.at[j, c], to).start()

    def key_wait(j, cs):
        rcopy(key_at(j, cs), key_at(j, cs), s_kf.at[0], r_k.at[j, cs], peer(dc=1)).wait_recv()
        rcopy(kmeta.at[j, cs], kmeta.at[j, cs], s_kmf.at[0], r_km.at[j, cs], peer(dc=1)).wait_recv()

    def key_share(j):
        rcopy(key_at(j, c), key_at(j, c), s_kf.at[j], r_k.at[j, c], peer(dc=1)).start()
        rcopy(kmeta.at[j, c], kmeta.at[j, c], s_kmf.at[j], r_km.at[j, c], peer(dc=1)).start()

    def key_codes(j):
        for cs in range(2):
            tile = kmeta[j, cs]
            code = (tile[0:1] - 1.0) * SPAN + tile[1:2]
            at = (j * 2 + cs) * CAP
            kcode[at:at + CAP, :] = jnp.transpose(jnp.broadcast_to(code, (128, CAP)))

    for k in (1, 3, 2):
        rows, tile = of_residue((y + k) % NY)
        ksel[k] = rows
        kmsrc[k] = tile
        key_send(k)
    rows, tile = of_residue(y)
    kbuf[pl.ds(pl.multiple_of(c * CAP, CAP), CAP)] = rows
    kmeta[0, c] = tile

    def x_start():
        for dx in (0, 1, 3, 2):
            xs = (x + dx) % NX
            runs_arrive(0, xs, xs, int(dx == 0))
            for step in (1, -1):
                along_z("x", dx, 0, step)

    def x_step(s):
        for dx in (0, 1, 3, 2):
            if s == 4:
                arrive(dx, 4)
                continue
            for dz in (-s, s):
                arrive(dx, dz)
                if s < 3:
                    along_z("x", dx, dz, 1 if dz < 0 else -1)
            if s == 3:
                across("x", dx)

    def z_start():
        for dz in (-1, 1, 0):
            runs_arrive(AT[dz], x, AT[dz], int(dz == 0))
            if dz != 0:
                along_z("z", 0, dz, -dz)
        for dz in (0, -1, 1):
            along_x(dz)

    def z_step(s):
        if s == 4:
            arrive(0, 4)
            along_x(4)
            return
        for dz in (-s, s):
            arrive(0, dz)
            if s < 3:
                along_z("z", 0, dz, 1 if dz < 0 else -1)
        if s == 3:
            across("z", 0)
        for dz in (-s, s):
            along_x(dz)

    def x_wait(s):
        for dz in ((s,) if s in (0, 4) else (-s, s)):
            for dx in (1, 3, 2):
                arrive(dx, dz)

    def rect(i0, i1, j0, j1):
        first, last = j0 * 2 * CAP, j1 * 2 * CAP
        s = lax.dot_general(
            kbuf[first:last], qbuf[i0 * NX * QB:i1 * NX * QB],
            (((1,), (1,)), ((), ())), preferred_element_type=F32,
        )
        code = kcode[first:last]
        for i in range(i0, i1):
            for p in range(2):
                tile = jnp.where(lane[0:2] < QB, qmeta[i, 2 * p], qmeta[i, 2 * p + 1])
                low = (tile[0:1] - 1.0) * SPAN
                high = low + tile[1:2]
                keep = (code >= low) & (code < high)
                at = ((i - i0) * 2 + p) * 128
                top = jnp.max(jnp.where(keep, s[:, at:at + 128], -1.0), axis=0, keepdims=True)
                best[i, p:p + 1, :] = jnp.maximum(best[i, p:p + 1, :], top)

    FAR = (0, -1, 1, -2, 2, -3, 3, 4)

    def slab_copy(i):
        return rcopy(best.at[i], zred.at[i], s_z.at[i], r_z.at[i], peer(dz=FAR[i]))

    HOME = [(k, dx) for dx in (2, 1, 3, 0) for k in (2, 1, 3, 0)]

    def home_copy(n, across):
        k, dx = HOME[n]
        if across:
            return rcopy(best.at[7], fin.at[1, y, x], s_l.at[n], r_f.at[1, y, x], peer(dy=k, dx=dx, dz=4))
        return rcopy(rtile, fin.at[0, y, x], s_f.at[n], r_f.at[0, y, x], peer(dy=k, dx=dx))

    best[...] = jnp.full(best.shape, -1.0, F32)

    def both(*steps):
        for step in steps:
            step()

    by_core(x_start, lambda: both(z_start, lambda: x_wait(0)))

    @pl.when(c == 0)
    def _():
        pl.semaphore_wait(beside, 1)

    key_share(0)
    key_wait(0, 1 - c)
    key_codes(0)
    rect(0, 1, 0, 1)
    by_core(lambda: x_step(1), lambda: both(lambda: z_step(2), lambda: x_wait(1)))
    rect(1, 3, 0, 1)
    for j in (1, 2):
        key_wait(j, c)
        key_share(j)
    by_core(lambda: x_step(2), lambda: both(lambda: z_step(3), lambda: x_wait(2), lambda: z_step(4)))
    for j in (1, 2):
        key_wait(j, 1 - c)
        key_codes(j)
    rect(0, 3, 1, 3)
    rect(3, 5, 0, 3)
    by_core(lambda: x_step(3), lambda: x_wait(3))
    rect(5, 7, 0, 3)
    key_wait(3, c)
    key_share(3)
    key_wait(3, 1 - c)
    key_codes(3)
    rect(0, 7, 3, 4)
    for i in range(1, 7):
        slab_copy(i).start()
    by_core(lambda: x_step(4), lambda: x_wait(4))
    rect(7, 8, 0, 4)

    for n in range(len(HOME)):
        home_copy(n, True).start()
    top = best[0]
    for i in range(1, 7):
        slab_copy(i).wait_recv()
        top = jnp.maximum(top, zred[i])
    rtile[...] = top
    for n in range(len(HOME) - 1):
        home_copy(n, False).start()
    fin[0, y, x] = top
    for k, dx in reversed(HOME):
        ys, xs = (y + k) % NY, (x + dx) % NX
        for q in range(2):
            if q == 1 or (k, dx) != (0, 0):
                rcopy(rtile, fin.at[q, ys, xs], s_f.at[0], r_f.at[q, ys, xs], peer(dc=1)).wait_recv()
    result = jnp.zeros((8, 128), F32)
    for r in range(NY):
        tile = jnp.max(fin[:, r].reshape(2 * NX, 2, 128), axis=0)
        tile = jnp.where(x // 2 == 0, tile[0:1], tile[1:2])
        tile = jnp.broadcast_to(tile, (8, 128))
        tile = pltpu.roll(tile, (r * RUN - (x % 2) * QB - ((y - r + NY) % NY) * RUN + 256) % 128, 1)
        result = jnp.where(lane // RUN == r, tile, result)
    out_ref[...] = result[0, 0:QB]

    def drain(runs, count):
        for n in range(runs):
            rcopy(qsel.at[pl.ds(0, RUN)], block_at(0, x, 0, RUN), s_q.at[n], r_q.at[0, 0], peer(dc=1)).wait_send()
            rcopy(qmsrc.at[0], qmrecv.at[0, 0], s_m.at[n], r_m.at[0, 0], peer(dc=1)).wait_send()
        for n in range(count):
            rcopy(block_at(0, x), block_at(0, x), s_g.at[n], r_g.at[0, x], peer(dc=1)).wait_send()
            rcopy(qmeta.at[0, x], qmeta.at[0, x], s_gm.at[n], r_gm.at[0, x], peer(dc=1)).wait_send()

    by_core(lambda: drain(len(X_RUNS), sent["x"]), lambda: drain(len(Z_RUNS), sent["z"]))
    for k in range(1, NY):
        rcopy(ksel.at[k], key_at(0, c), s_k.at[k], r_k.at[0, c], peer(dy=k)).wait_send()
        rcopy(kmsrc.at[k], kmeta.at[0, c], s_km.at[k], r_km.at[0, c], peer(dy=k)).wait_send()
    for j in range(NY):
        rcopy(key_at(j, c), key_at(j, c), s_kf.at[j], r_k.at[j, c], peer(dc=1)).wait_send()
        rcopy(kmeta.at[j, c], kmeta.at[j, c], s_kmf.at[j], r_km.at[j, c], peer(dc=1)).wait_send()
    for i in range(1, 7):
        slab_copy(i).wait_send()
    for n in range(len(HOME)):
        home_copy(n, True).wait_send()
        if n < len(HOME) - 1:
            home_copy(n, False).wait_send()


def body(embeddings, cluster, order, query_local):
    dma = pltpu.SemaphoreType.DMA
    out = pl.pallas_call(
        kernel,
        out_shape=jax.ShapeDtypeStruct((QB,), F32),
        in_specs=[pl.BlockSpec(memory_space=pl.ANY)] * 4,
        out_specs=pl.BlockSpec(memory_space=pltpu.VMEM),
        scratch_shapes=[
            pltpu.VMEM((ROWS, D), BF16),
            pltpu.VMEM((1, ROWS), jnp.int32),
            pltpu.VMEM((1, ROWS), jnp.int32),
            pltpu.VMEM((1, QB), jnp.int32),
            pltpu.VMEM((ROWS, D), BF16),
            pltpu.VMEM((QB, D), BF16),
            pltpu.VMEM((NY, 2, 128), F32),
            pltpu.VMEM((NX, NY, 2, 128), F32),
            pltpu.VMEM((NY, CAP, D), BF16),
            pltpu.VMEM((NY, 2, CAP), F32),
            pltpu.VMEM((NY * 2 * CAP, D), BF16),
            pltpu.VMEM((NY, 2, 2, CAP), F32),
            pltpu.VMEM((NY * 2 * CAP, 128), F32),
            pltpu.VMEM((NZ * NX * QB, D), BF16),
            pltpu.VMEM((NZ, NX, 2, 128), F32),
            pltpu.VMEM((NZ, 2, 128), F32),
            pltpu.VMEM((NZ, 2, 128), F32),
            pltpu.VMEM((2, 128), F32),
            pltpu.VMEM((2, NY, NX, 2, 128), F32),
            dma((4,)), dma((15,)), dma((15,)), dma((NX, NY)), dma((NX, NY)),
            dma((NY,)), dma((NY,)), dma((NY, 2)), dma((NY, 2)), dma((NY,)), dma((NY,)),
            dma((29,)), dma((29,)), dma((NZ, NX)), dma((NZ, NX)),
            dma((NZ,)), dma((NZ,)), dma((NY * NX,)), dma((2, NY, NX)), dma((NY * NX,)),
            pltpu.SemaphoreType.REGULAR,
        ],
        compiler_params=pltpu.CompilerParams(
            collective_id=0, has_side_effects=True, vmem_limit_bytes=56 * 1024 * 1024
        ),
        name="dedup",
    )(
        embeddings,
        cluster.reshape(1, ROWS),
        order.reshape(1, ROWS),
        query_local.reshape(1, QB),
    )
    return out


def solution(mesh):
    return jax.shard_map(
        body,
        mesh=mesh,
        in_specs=(
            P(("group", "dev"), None),
            P(("group", "dev")),
            P(("group", "dev")),
            P(("group", "dev")),
        ),
        out_specs=P(("group", "dev")),
        check_vma=False,
    )
```

time: 685 us -> 53.7 us (0.08)
  waiting for transfers between devices: 616 us -> 0 us
  Pallas kernels: 0 us -> 52.4 us
  matrix products: 41.1 us -> 0 us
  between operations: 13.2 us -> 0.01 us
  local copies, waits for them, and re-layouts: 11.2 us -> 1.19 us
    unnamed x4 -> x0, waiting for transfers between devices: 243 us -> none
    pmax x1 -> x0, waiting for transfers between devices: 235 us -> none  [body(): total = lax.pmax(partial_value, ('group', 'dev'))]
    all_gather x1 -> x0, waiting for transfers between devices: 138 us -> none  [body(): lax.all_gather(own_rows, ('group', 'dev'), axis=0, tiled=True)]
    pallas_call x0 -> x1, Pallas kernels: none -> 52.4 us  [body(): pl.pallas_call(kernel, out_shape=jax.ShapeDtypeStruct((QB,), F32), in_spe...]
    dot_general x16 -> x0, matrix products: 41.1 us -> none  [tile_best(): lax.dot_general(rows, keys, (((1,), (1,)), ((), ())), preferred_element_t...]
  transfers between devices with their start and end apart: 3 -> 0, of which waited for: 3 -> 0; matrix products, arithmetic and copies ran while one was open for 1% -> 0% of each run, Pallas kernels for 0% -> 0%
where the time goes in v2:
time: 53.7 us; the launch traced here: 53.6 us
  Pallas kernels  52.4 us (98%)
  local copies, waits for them, and re-layouts  1.19 us (2%)
    pallas_call x1, Pallas kernels, body(): pl.pallas_call(kernel, out_shape=jax.ShapeDtypeStruct((QB,), F32), in_spe...  52.4 us
    unnamed x1, local copies, waits for them, and re-layouts  1.19 us

profile of v2, /device:TPU:1, one launch (start us, length us, event | category | flops | bytes accessed | tf_op | source)
XLA Modules:
  0.0 53.6 jit_solution(10118205913440023105)
XLA Ops:
  0.0 52.4 %dedup.1 = f32[64]{0:T(128)} custom-call(bf16[512,768]{1,0:T(8,128)(2,1)} %emb_hbm.1, s32[1,512]{1,0:T(1,128)} %bitcast.3, s32[1,512]{1,0:T(1,128)} %bitcast.4, s32[1,64]{1,0:T(1,128)} %bitcast.5), custom_call_target="tpu_custom_call" | custom-call | tf_op jit(solution)/shard_map/dedup/pallas_call | solution.py:394
  52.4 1.2 %copy.6 = f32[64]{0:T(128)} copy(f32[64]{0:T(128)} %dedup.1) | data formatting | bytes 512

commit v3 on v2

--- a/solution.py
+++ b/solution.py
@@ -148,8 +148,8 @@
         rcopy(block_at(at, xs), block_at(at, xs), s_g.at[0], r_g.at[at, xs], peer(dc=1)).wait_recv()
         rcopy(qmeta.at[at, xs], qmeta.at[at, xs], s_gm.at[0], r_gm.at[at, xs], peer(dc=1)).wait_recv()
 
-    X_RUNS = [(k, dx) for dx in (2, 1, 3, 0) for k in (2, 1, 3, 0) if (k, dx) != (0, 0)]
-    Z_RUNS = [(k, dz) for dz in (1, -1, 0) for k in (2, 1, 3, 0) if (k, dz) != (0, 0)]
+    X_RUNS = [(k, dx) for dx in (0, 1, 3, 2) for k in (2, 1, 3, 0) if (k, dx) != (0, 0)]
+    Z_RUNS = [(k, dz) for dz in (0, 1, -1) for k in (2, 1, 3, 0) if (k, dz) != (0, 0)]
 
     def run_send(n, k, at, slot, to):
         i, back = (y + k) % NY, (NY - k) % NY
@@ -247,11 +247,13 @@
                 across("x", dx)
 
     def z_start():
-        for dz in (-1, 1, 0):
+        for dz in (0, -1, 1):
             runs_arrive(AT[dz], x, AT[dz], int(dz == 0))
+            if dz == 0:
+                along_x(0)
             if dz != 0:
                 along_z("z", 0, dz, -dz)
-        for dz in (0, -1, 1):
+        for dz in (-1, 1):
             along_x(dz)
 
     def z_step(s):
@@ -309,7 +311,7 @@
         for step in steps:
             step()
 
-    by_core(x_start, lambda: both(z_start, lambda: x_wait(0)))
+    by_core(x_start, lambda: both(z_start, lambda: z_step(2), lambda: x_wait(0)))
 
     @pl.when(c == 0)
     def _():
@@ -319,21 +321,22 @@
     key_wait(0, 1 - c)
     key_codes(0)
     rect(0, 1, 0, 1)
-    by_core(lambda: x_step(1), lambda: both(lambda: z_step(2), lambda: x_wait(1)))
+    by_core(lambda: x_step(1), lambda: both(lambda: z_step(3), lambda: x_wait(1)))
     rect(1, 3, 0, 1)
     for j in (1, 2):
         key_wait(j, c)
         key_share(j)
-    by_core(lambda: x_step(2), lambda: both(lambda: z_step(3), lambda: x_wait(2), lambda: z_step(4)))
+    by_core(lambda: x_step(2), lambda: both(lambda: z_step(4), lambda: x_wait(2)))
     for j in (1, 2):
         key_wait(j, 1 - c)
         key_codes(j)
     rect(0, 3, 1, 3)
     rect(3, 5, 0, 3)
-    by_core(lambda: x_step(3), lambda: x_wait(3))
-    rect(5, 7, 0, 3)
+    by_core(lambda: x_step(3), lambda: None)
     key_wait(3, c)
     key_share(3)
+    by_core(lambda: None, lambda: x_wait(3))
+    rect(5, 7, 0, 3)
     key_wait(3, 1 - c)
     key_codes(3)
     rect(0, 7, 3, 4)
@@ -351,6 +354,23 @@
     rtile[...] = top
     for n in range(len(HOME) - 1):
         home_copy(n, False).start()
+    def drain(runs, count):
+        for n in range(runs):
+            rcopy(qsel.at[pl.ds(0, RUN)], block_at(0, x, 0, RUN), s_q.at[n], r_q.at[0, 0], peer(dc=1)).wait_send()
+            rcopy(qmsrc.at[0], qmrecv.at[0, 0], s_m.at[n], r_m.at[0, 0], peer(dc=1)).wait_send()
+        for n in range(count):
+            rcopy(block_at(0, x), block_at(0, x), s_g.at[n], r_g.at[0, x], peer(dc=1)).wait_send()
+            rcopy(qmeta.at[0, x], qmeta.at[0, x], s_gm.at[n], r_gm.at[0, x], peer(dc=1)).wait_send()
+
+    by_core(lambda: drain(len(X_RUNS), sent["x"]), lambda: drain(len(Z_RUNS), sent["z"]))
+    for k in range(1, NY):
+        rcopy(ksel.at[k], key_at(0, c), s_k.at[k], r_k.at[0, c], peer(dy=k)).wait_send()
+        rcopy(kmsrc.at[k], kmeta.at[0, c], s_km.at[k], r_km.at[0, c], peer(dy=k)).wait_send()
+    for j in range(NY):
+        rcopy(key_at(j, c), key_at(j, c), s_kf.at[j], r_k.at[j, c], peer(dc=1)).wait_send()
+        rcopy(kmeta.at[j, c], kmeta.at[j, c], s_kmf.at[j], r_km.at[j, c], peer(dc=1)).wait_send()
+    for i in range(1, 7):
+        slab_copy(i).wait_send()
     fin[0, y, x] = top
     for k, dx in reversed(HOME):
         ys, xs = (y + k) % NY, (x + dx) % NX
@@ -366,23 +386,6 @@
         result = jnp.where(lane // RUN == r, tile, result)
     out_ref[...] = result[0, 0:QB]
 
-    def drain(runs, count):
-        for n in range(runs):
-            rcopy(qsel.at[pl.ds(0, RUN)], block_at(0, x, 0, RUN), s_q.at[n], r_q.at[0, 0], peer(dc=1)).wait_send()
-            rcopy(qmsrc.at[0], qmrecv.at[0, 0], s_m.at[n], r_m.at[0, 0], peer(dc=1)).wait_send()
-        for n in range(count):
-            rcopy(block_at(0, x), block_at(0, x), s_g.at[n], r_g.at[0, x], peer(dc=1)).wait_send()
-            rcopy(qmeta.at[0, x], qmeta.at[0, x], s_gm.at[n], r_gm.at[0, x], peer(dc=1)).wait_send()
-
-    by_core(lambda: drain(len(X_RUNS), sent["x"]), lambda: drain(len(Z_RUNS), sent["z"]))
-    for k in range(1, NY):
-        rcopy(ksel.at[k], key_at(0, c), s_k.at[k], r_k.at[0, c], peer(dy=k)).wait_send()
-        rcopy(kmsrc.at[k], kmeta.at[0, c], s_km.at[k], r_km.at[0, c], peer(dy=k)).wait_send()
-    for j in range(NY):
-        rcopy(key_at(j, c), key_at(j, c), s_kf.at[j], r_k.at[j, c], peer(dc=1)).wait_send()
-        rcopy(kmeta.at[j, c], kmeta.at[j, c], s_kmf.at[j], r_km.at[j, c], peer(dc=1)).wait_send()
-    for i in range(1, 7):
-        slab_copy(i).wait_send()
     for n in range(len(HOME)):
         home_copy(n, True).wait_send()
         if n < len(HOME) - 1:

time: 53.7 us -> 52.4 us (0.976)
  Pallas kernels: 52.4 us -> 51.1 us
    pallas_call x1, Pallas kernels: 52.4 us -> 51.1 us  [body(): pl.pallas_call(kernel, out_shape=jax.ShapeDtypeStruct((QB,), F32), in_spe...]
where the time goes in v3:
time: 52.4 us; the launch traced here: 52.3 us
  Pallas kernels  51.1 us (98%)
  local copies, waits for them, and re-layouts  1.19 us (2%)
    pallas_call x1, Pallas kernels, body(): pl.pallas_call(kernel, out_shape=jax.ShapeDtypeStruct((QB,), F32), in_spe...  51.1 us
    unnamed x1, local copies, waits for them, and re-layouts  1.19 us

profile of v3, /device:TPU:1, one launch (start us, length us, event | category | flops | bytes accessed | tf_op | source)
XLA Modules:
  0.0 52.3 jit_solution(14369676006094426243)
XLA Ops:
  0.0 51.1 %dedup.1 = f32[64]{0:T(128)} custom-call(bf16[512,768]{1,0:T(8,128)(2,1)} %emb_hbm.1, s32[1,512]{1,0:T(1,128)} %bitcast.3, s32[1,512]{1,0:T(1,128)} %bitcast.4, s32[1,64]{1,0:T(1,128)} %bitcast.5), custom_call_target="tpu_custom_call" | custom-call | tf_op jit(solution)/shard_map/dedup/pallas_call | solution.py:397
  51.1 1.2 %copy.6 = f32[64]{0:T(128)} copy(f32[64]{0:T(128)} %dedup.1) | data formatting | bytes 512

commit v4 on v3

--- a/solution.py
+++ b/solution.py
@@ -426,7 +426,7 @@
             pltpu.SemaphoreType.REGULAR,
         ],
         compiler_params=pltpu.CompilerParams(
-            collective_id=0, has_side_effects=True, vmem_limit_bytes=56 * 1024 * 1024
+            collective_id=0, has_side_effects=True, vmem_limit_bytes=54912 * 1024
         ),
         name="dedup",
     )(

time: 52.4 us -> 52 us (level)
    unnamed x1 -> x7, local copies, waits for them, and re-layouts: 1.19 us -> 1.21 us
where the time goes in v4:
time: 52 us; the launch traced here: 51.8 us
  Pallas kernels  50.6 us (97%)
  local copies, waits for them, and re-layouts  1.21 us (2%)
    pallas_call x1, Pallas kernels, body(): pl.pallas_call(kernel, out_shape=jax.ShapeDtypeStruct((QB,), F32), in_spe...  50.6 us
    unnamed x7, local copies, waits for them, and re-layouts  1.21 us

profile of v4, /device:TPU:1, one launch (start us, length us, event | category | flops | bytes accessed | tf_op | source)
XLA Modules:
  0.0 51.8 jit_solution(2355205243151284402)
XLA Ops:
  0.0 0.0 copy-start.1
  0.0 0.0 copy-start
  0.0 0.0 copy-start.2
  0.0 0.7 %copy-done.1 = s32[512]{0:T(512)S(1)} copy-done((s32[512]{0:T(512)S(1)}, s32[512]{0:T(512)}, u32[]{:S(2)}) %copy-start.1) | copy-done | bytes 2072
  0.7 0.0 copy-done
  0.7 0.0 copy-done.2
  0.7 50.6 %dedup.1 = f32[64]{0:T(128)S(1)} custom-call(bf16[512,768]{1,0:T(8,128)(2,1)} %emb_hbm.1, s32[1,512]{1,0:T(1,128)S(1)} %bitcast.3, s32[1,512]{1,0:T(1,128)S(1)} %bitcast.4, s32[1,64]{1,0:T(1,128)S(1)} %bitcast.5), custom_call_target="tpu_custom_call" | custom-call | tf_op jit(solution)/shard_map/dedup/pallas_call | solution.py:397
  51.3 0.5 copy.6
Async XLA Ops:
  0.0 0.7 %copy-start.1 = (s32[512]{0:T(512)S(1)}, s32[512]{0:T(512)}, u32[]{:S(2)}) copy-start(s32[512]{0:T(512)} %param.6) | copy-start | bytes 6148
  0.0 0.7 %copy-start = (s32[512]{0:T(512)S(1)}, s32[512]{0:T(512)}, u32[]{:S(2)}) copy-start(s32[512]{0:T(512)} %param.5) | copy-start | bytes 6148
  0.0 0.7 %copy-start.2 = (s32[64]{0:T(128)S(1)}, s32[64]{0:T(128)}, u32[]{:S(2)}) copy-start(s32[64]{0:T(128)} %param.7) | copy-start | bytes 772

commit v5 on v4

--- a/solution.py
+++ b/solution.py
@@ -136,7 +136,7 @@
         send(who, dx, AT[dz], AT[dz - step], peer(dz=step))
 
     def along_x(dz):
-        for dx in (1, 3, 2):
+        for dx in (2, 1, 3):
             send("z", 0, AT[dz], AT[dz], peer(dx=dx))
 
     def across(who, dx):

time: 52 us -> 51.4 us (0.988)
  Pallas kernels: 50.6 us -> 50 us
    pallas_call x1, Pallas kernels: 50.6 us -> 50 us  [body(): pl.pallas_call(kernel, out_shape=jax.ShapeDtypeStruct((QB,), F32), in_spe...]
where the time goes in v5:
time: 51.4 us; the launch traced here: 51.2 us
  Pallas kernels  50 us (97%)
  local copies, waits for them, and re-layouts  1.21 us (2%)
    pallas_call x1, Pallas kernels, body(): pl.pallas_call(kernel, out_shape=jax.ShapeDtypeStruct((QB,), F32), in_spe...  50 us
    unnamed x7, local copies, waits for them, and re-layouts  1.21 us

profile of v5, /device:TPU:1, one launch (start us, length us, event | category | flops | bytes accessed | tf_op | source)
XLA Modules:
  0.0 51.2 jit_solution(2796062917005171776)
XLA Ops:
  0.0 0.0 copy-start.1
  0.0 0.0 copy-start
  0.0 0.0 copy-start.2
  0.0 0.7 %copy-done.1 = s32[512]{0:T(512)S(1)} copy-done((s32[512]{0:T(512)S(1)}, s32[512]{0:T(512)}, u32[]{:S(2)}) %copy-start.1) | copy-done | bytes 2072
  0.7 0.0 copy-done
  0.7 0.0 copy-done.2
  0.7 50.0 %dedup.1 = f32[64]{0:T(128)S(1)} custom-call(bf16[512,768]{1,0:T(8,128)(2,1)} %emb_hbm.1, s32[1,512]{1,0:T(1,128)S(1)} %bitcast.3, s32[1,512]{1,0:T(1,128)S(1)} %bitcast.4, s32[1,64]{1,0:T(1,128)S(1)} %bitcast.5), custom_call_target="tpu_custom_call" | custom-call | tf_op jit(solution)/shard_map/dedup/pallas_call | solution.py:397
  50.7 0.5 %copy.6 = f32[64]{0:T(128)} copy(f32[64]{0:T(128)S(1)} %dedup.1) | data formatting | bytes 512
Async XLA Ops:
  0.0 0.7 %copy-start.1 = (s32[512]{0:T(512)S(1)}, s32[512]{0:T(512)}, u32[]{:S(2)}) copy-start(s32[512]{0:T(512)} %param.6) | copy-start | bytes 6148
  0.0 0.7 %copy-start = (s32[512]{0:T(512)S(1)}, s32[512]{0:T(512)}, u32[]{:S(2)}) copy-start(s32[512]{0:T(512)} %param.5) | copy-start | bytes 6148
  0.0 0.7 %copy-start.2 = (s32[64]{0:T(128)S(1)}, s32[64]{0:T(128)}, u32[]{:S(2)}) copy-start(s32[64]{0:T(128)} %param.7) | copy-start | bytes 772

commit v6 on v5

--- a/solution.py
+++ b/solution.py
@@ -218,14 +218,18 @@
             at = (j * 2 + cs) * CAP
             kcode[at:at + CAP, :] = jnp.transpose(jnp.broadcast_to(code, (128, CAP)))
 
-    for k in (1, 3, 2):
+    def key_begin(k):
         rows, tile = of_residue((y + k) % NY)
         ksel[k] = rows
         kmsrc[k] = tile
         key_send(k)
+
+    key_begin(1)
+    key_begin(3)
     rows, tile = of_residue(y)
     kbuf[pl.ds(pl.multiple_of(c * CAP, CAP), CAP)] = rows
     kmeta[0, c] = tile
+    key_begin(2)
 
     def x_start():
         for dx in (0, 1, 3, 2):

time: 51.4 us -> 51.4 us (level)
  no operation moved by 1% of the time
where the time goes in v6:
time: 51.4 us; the launch traced here: 51.2 us
  Pallas kernels  50 us (97%)
  local copies, waits for them, and re-layouts  1.21 us (2%)
    pallas_call x1, Pallas kernels, body(): pl.pallas_call(kernel, out_shape=jax.ShapeDtypeStruct((QB,), F32), in_spe...  50 us
    unnamed x7, local copies, waits for them, and re-layouts  1.21 us

profile of v6, /device:TPU:1, one launch (start us, length us, event | category | flops | bytes accessed | tf_op | source)
XLA Modules:
  0.0 51.2 jit_solution(5246900013110895557)
XLA Ops:
  0.0 0.0 copy-start.1
  0.0 0.0 copy-start
  0.0 0.0 copy-start.2
  0.0 0.7 %copy-done.1 = s32[512]{0:T(512)S(1)} copy-done((s32[512]{0:T(512)S(1)}, s32[512]{0:T(512)}, u32[]{:S(2)}) %copy-start.1) | copy-done | bytes 2072
  0.7 0.0 copy-done
  0.7 0.0 copy-done.2
  0.7 50.0 %dedup.1 = f32[64]{0:T(128)S(1)} custom-call(bf16[512,768]{1,0:T(8,128)(2,1)} %emb_hbm.1, s32[1,512]{1,0:T(1,128)S(1)} %bitcast.3, s32[1,512]{1,0:T(1,128)S(1)} %bitcast.4, s32[1,64]{1,0:T(1,128)S(1)} %bitcast.5), custom_call_target="tpu_custom_call" | custom-call | tf_op jit(solution)/shard_map/dedup/pallas_call | solution.py:401
  50.7 0.5 %copy.6 = f32[64]{0:T(128)} copy(f32[64]{0:T(128)S(1)} %dedup.1) | data formatting | bytes 512
Async XLA Ops:
  0.0 0.7 %copy-start.1 = (s32[512]{0:T(512)S(1)}, s32[512]{0:T(512)}, u32[]{:S(2)}) copy-start(s32[512]{0:T(512)} %param.6) | copy-start | bytes 6148
  0.0 0.7 %copy-start = (s32[512]{0:T(512)S(1)}, s32[512]{0:T(512)}, u32[]{:S(2)}) copy-start(s32[512]{0:T(512)} %param.5) | copy-start | bytes 6148
  0.0 0.7 %copy-start.2 = (s32[64]{0:T(128)S(1)}, s32[64]{0:T(128)}, u32[]{:S(2)}) copy-start(s32[64]{0:T(128)} %param.7) | copy-start | bytes 772
